TPU v7x, 256 devices: a whole 4x4x8 slice. The times are simulated.
256 devices in a mesh: dp: 16 (over y_lo, z), section: 16 (over y_hi, x, core).
Axes of the slice: x: 4, y: 4 (y_hi: 2, y_lo: 2; y = y_hi * 2 + y_lo), z: 8, core: 2. Of those that a mesh axis runs over, the one named last changes fastest.
Arguments:
- section_inputs: bfloat16 [16, 4096, 2048], P('section', 'dp'), may hold values from -160 to 160
- enc_output: bfloat16 [4096, 2048], P('dp'), may hold values from -160 to 160
- attention_probs: bfloat16 [16, 128, 8, 32, 32], P('section', 'dp'), may hold values from 0 to 1, as said below
- value_weight: bfloat16 [16, 2048, 1024], P('section', 'dp'), may hold values from -0.125 to 0.125
- out_weight: bfloat16 [16, 1024, 2048], P('section', None, 'dp'), may hold values from -0.1875 to 0.1875
- norm_gain: float32 [16, 2048], P('section'), may hold values from 0.1 to 1.9
- top_grad: bfloat16 [4096, 2048], P('dp'), may hold values from -6 to 6
- enc_sentinel: int32 [128, 32], P('dp'), may hold values from 0 to 100, as said below
- dec_sentinel: int32 [128, 32], P('dp'), may hold values from 0 to 100, as said below
Outputs:
- section_input_grad: bfloat16 [16, 4096, 2048], P('section', 'dp')
- score_grad: bfloat16 [16, 128, 8, 32, 32], P('section', 'dp')
- value_weight_grad: bfloat16 [16, 2048, 1024], P('section', 'dp')
- out_weight_grad: bfloat16 [16, 1024, 2048], P('section', None, 'dp')
- gain_grad: float32 [16, 2048], P('section', 'dp')
- sentinel_grad: float32 [100, 2048], P(None, ('dp', 'section'))
Inputs may be any that keep to these rules, and one draw needn't show every extreme that they name: `enc_sentinel`: along each sequence the positions that hold a sentinel carry the numbers 0, 1, 2, ... in order; the first position holds sentinel 0; 100 marks a position without a sentinel. `dec_sentinel`: along each sequence the positions that hold a sentinel carry the numbers 0, 1, 2, ... in order; the first position holds sentinel 0; 100 marks a position without a sentinel. `attention_probs`: each row over keys is a probability distribution, up to rounding.
All inputs are finite; a program needn't handle non-finite values.
Results may differ from a plain program's by a relative error of at most 0.027.
Values may be sent and summed in bfloat16 or wider, within the bound.
No kernel may reach another device: no remote copies, remote signals or barrier semaphores. Data moves between devices by JAX's collectives and lax.ppermute only.
A program may use at most 64 MiB of HBM per device.

v0:
```python
import jax
import jax.numpy as jnp
from jax import lax
from jax.sharding import PartitionSpec as P

SENT = 100


epsilon = 1e-06


def shifted(block, axis, distance):
    devices = range(lax.axis_size(axis))
    route = [(i - distance, i) for i in devices if i - distance in devices]
    return lax.ppermute(block, axis, route)


def passed_along(block, axis, distance):
    devices = range(lax.axis_size(axis))
    route = [((i - distance) % len(devices), i) for i in devices]
    return lax.ppermute(block, axis, route)


def norm_parts(source, gain_row):
    widened = source.astype(jnp.float32)
    inverse = lax.rsqrt(jnp.mean(widened * widened, axis=-1, keepdims=True) + epsilon)
    unit_rows = widened * inverse
    return (inverse, unit_rows, (unit_rows * gain_row).astype(jnp.bfloat16))


def section_backward(out_grad, source, prob_block, gain_row, w_value, w_out, head_count):
    seq_length = source.shape[0]
    inverse, unit_rows, normed = norm_parts(source, gain_row)
    values = jnp.dot(normed, w_value, preferred_element_type=jnp.float32).astype(jnp.bfloat16)
    head_values = values.reshape(seq_length, head_count, -1)
    context = jnp.einsum(
        "hqk,khd->qhd", prob_block, head_values, preferred_element_type=jnp.float32
    )
    context = context.astype(jnp.bfloat16).reshape(seq_length, -1)
    ctx_grad = jnp.einsum("qd,id->qi", out_grad, w_out, preferred_element_type=jnp.float32).astype(
        jnp.bfloat16
    )
    head_grads = ctx_grad.reshape(seq_length, head_count, -1)
    prob_grad = jnp.einsum(
        "qhd,khd->hqk", head_grads, head_values, preferred_element_type=jnp.float32
    )
    prob_wide = prob_block.astype(jnp.float32)
    score_grad = (
        prob_wide * (prob_grad - jnp.sum(prob_grad * prob_wide, axis=-1, keepdims=True))
    ).astype(jnp.bfloat16)
    value_grad = jnp.einsum(
        "hqk,qhd->khd", prob_block, head_grads, preferred_element_type=jnp.float32
    )
    value_grad = value_grad.astype(jnp.bfloat16).reshape(seq_length, -1)
    normed_grad = jnp.einsum("ki,di->kd", value_grad, w_value, preferred_element_type=jnp.float32)
    scaled = normed_grad * gain_row
    source_grad = inverse * (
        scaled - unit_rows * jnp.mean(scaled * unit_rows, axis=-1, keepdims=True)
    )
    gain_term = jnp.sum(normed_grad * unit_rows, axis=0)
    return (normed, context, value_grad, score_grad, source_grad, gain_term)


def pass_down(in_grad):
    return shifted(in_grad, "section", -1)


def body(
    section_inputs,
    enc_output,
    attention_probs,
    value_weight,
    out_weight,
    norm_gain,
    top_grad,
    enc_sentinel,
    dec_sentinel,
):
    section_count = lax.axis_size("section")
    half_point = section_count // 2
    section_index = lax.axis_index("section")
    is_cross = jnp.logical_and(section_index >= half_point, (section_index - half_point) % 2 == 1)
    full_value, full_out = (
        lax.all_gather(value_weight, "dp", axis=1, tiled=True),
        lax.all_gather(out_weight, "dp", axis=2, tiled=True),
    )
    w_value = full_value[0]
    w_out = full_out[0]
    gain_row = norm_gain[0]
    micro_count, seq_length = enc_sentinel.shape
    model_width = section_inputs.shape[2]
    inner_width = w_value.shape[1]
    head_count = attention_probs.shape[2]
    own_rows = section_inputs[0].reshape(micro_count, seq_length, model_width)
    sources = jnp.where(
        is_cross, enc_output.reshape(micro_count, seq_length, model_width), own_rows
    )
    prob_blocks = attention_probs[0]
    top_blocks = top_grad.reshape(micro_count, seq_length, model_width)
    block_shape = (micro_count, seq_length, model_width)
    buffers = (
        jnp.zeros(block_shape, jnp.bfloat16),
        jnp.zeros(block_shape, jnp.bfloat16),
        jnp.zeros(block_shape, jnp.bfloat16),
        jnp.zeros((micro_count, seq_length, inner_width), jnp.bfloat16),
        jnp.zeros((micro_count, seq_length, inner_width), jnp.bfloat16),
        jnp.zeros(prob_blocks.shape, jnp.bfloat16),
        jnp.zeros(block_shape, jnp.float32),
        jnp.zeros((model_width,), jnp.float32),
    )
    row_zeros = jnp.zeros((seq_length, model_width), jnp.bfloat16)
    wide_zeros = jnp.zeros((seq_length, model_width), jnp.float32)

    def run_micro(buffers, slot_index, out_grad, active):

        def work_branch(buffers):
            source = lax.dynamic_index_in_dim(sources, slot_index, 0, keepdims=False)
            prob_block = lax.dynamic_index_in_dim(prob_blocks, slot_index, 0, keepdims=False)
            normed, context, value_grad, score_grad, source_grad, gain_term = section_backward(
                out_grad, source, prob_block, gain_row, w_value, w_out, head_count
            )
            widened = out_grad.astype(jnp.float32)
            in_grad = jnp.where(is_cross, widened, widened + source_grad).astype(jnp.bfloat16)
            partial_value = jnp.where(is_cross, source_grad, 0.0)
            pieces = (in_grad, out_grad, normed, context, value_grad, score_grad, partial_value)
            stored = tuple(
                (
                    lax.dynamic_update_index_in_dim(buffer, new_piece, slot_index, 0)
                    for buffer, new_piece in zip(buffers[:7], pieces)
                )
            )
            return (stored + (buffers[7] + gain_term,), in_grad)

        def spare_branch(buffers):
            return (buffers, row_zeros)

        return lax.cond(active, work_branch, spare_branch, buffers)

    def decoder_step(step_number, carried):
        buffers, stream_grad = carried
        raw_slot = step_number - (section_count - 1 - section_index)
        slot_index = jnp.clip(raw_slot, 0, micro_count - 1)
        active = jnp.logical_and(
            section_index >= half_point, jnp.logical_and(raw_slot >= 0, raw_slot < micro_count)
        )
        top_block = lax.dynamic_index_in_dim(top_blocks, slot_index, 0, keepdims=False)
        out_grad = jnp.where(section_index == section_count - 1, top_block, stream_grad)
        buffers, in_grad = run_micro(buffers, slot_index, out_grad, active)
        return (buffers, pass_down(in_grad))

    buffers, stream_grad = lax.fori_loop(
        0, micro_count + half_point - 1, decoder_step, (buffers, row_zeros)
    )
    distance = (section_index - half_point) % section_count

    def chain_step(step_number, carried):
        side_grad, totals = carried
        raw_slot = step_number - distance
        valid = jnp.logical_and(raw_slot >= 0, raw_slot < micro_count)
        slot_index = jnp.clip(raw_slot, 0, micro_count - 1)
        incoming = jnp.where(section_index == half_point, 0.0, side_grad)
        own_part = lax.dynamic_index_in_dim(buffers[6], slot_index, 0, keepdims=False)
        running = incoming + jnp.where(valid, own_part, 0.0)
        keep_slot = jnp.logical_and(valid, section_index == half_point - 1)
        current = lax.dynamic_index_in_dim(totals, slot_index, 0, keepdims=False)
        totals = lax.dynamic_update_index_in_dim(
            totals, jnp.where(keep_slot, running, current), slot_index, 0
        )
        side_grad = passed_along(running.astype(jnp.bfloat16), "section", 1).astype(running.dtype)
        return (side_grad, totals)

    side_grad, totals = lax.fori_loop(
        0,
        micro_count + section_count - 1,
        chain_step,
        (wide_zeros, jnp.zeros(block_shape, jnp.float32)),
    )

    def encoder_step(step_number, carried):
        buffers, stream_grad = carried
        raw_slot = step_number - (half_point - 1 - section_index)
        slot_index = jnp.clip(raw_slot, 0, micro_count - 1)
        active = jnp.logical_and(
            section_index < half_point, jnp.logical_and(raw_slot >= 0, raw_slot < micro_count)
        )
        top_block = lax.dynamic_index_in_dim(totals, slot_index, 0, keepdims=False).astype(
            jnp.bfloat16
        )
        out_grad = jnp.where(section_index == half_point - 1, top_block, stream_grad)
        buffers, in_grad = run_micro(buffers, slot_index, out_grad, active)
        return (buffers, pass_down(in_grad))

    buffers, stream_grad = lax.fori_loop(
        0, micro_count + half_point - 1, encoder_step, (buffers, row_zeros)
    )
    in_rows = buffers[0].reshape(-1, model_width)
    chosen = jnp.where(
        section_index == 0, enc_sentinel, jnp.where(section_index == half_point, dec_sentinel, SENT)
    )
    onehot_table = (chosen.reshape(1, -1) == jnp.arange(SENT, dtype=jnp.int32)[:, None]).astype(
        jnp.bfloat16
    )
    sentinel_term = jnp.dot(onehot_table, in_rows, preferred_element_type=jnp.float32)
    sentinel_grad = lax.psum_scatter(
        sentinel_term, ("dp", "section"), scatter_dimension=1, tiled=True
    )
    out_rows = buffers[1].reshape(-1, model_width)
    normed_rows = buffers[2].reshape(-1, model_width)
    context_rows = buffers[3].reshape(-1, inner_width)
    value_rows = buffers[4].reshape(-1, inner_width)
    value_term = jnp.einsum(
        "td,ti->di", normed_rows, value_rows, preferred_element_type=jnp.float32
    )
    output_term = jnp.einsum(
        "td,ti->di", out_rows, context_rows, preferred_element_type=jnp.float32
    )
    value_sum, output_sum, gain_sum = (
        lax.psum_scatter(
            value_term.astype(jnp.bfloat16), "dp", scatter_dimension=0, tiled=True
        ).astype(jnp.float32),
        lax.psum_scatter(
            output_term.astype(jnp.bfloat16), "dp", scatter_dimension=0, tiled=True
        ).astype(jnp.float32),
        lax.psum_scatter(
            buffers[7].astype(jnp.bfloat16), "dp", scatter_dimension=0, tiled=True
        ).astype(jnp.float32),
    )
    return (
        in_rows.reshape(1, -1, model_width),
        buffers[5][None],
        value_sum.astype(jnp.bfloat16)[None],
        output_sum.T.astype(jnp.bfloat16)[None],
        gain_sum[None],
        sentinel_grad,
    )


def solution(mesh):
    placed = (
        P("section", "dp", None),
        P("dp", None),
        P("section", "dp", None, None, None),
        P("section", "dp", None),
        P("section", None, "dp"),
        P("section", None),
        P("dp", None),
        P("dp", None),
        P("dp", None),
    )
    return jax.shard_map(
        body,
        mesh=mesh,
        in_specs=placed,
        out_specs=(
            P("section", "dp", None),
            P("section", "dp", None, None, None),
            P("section", "dp", None),
            P("section", None, "dp"),
            P("section", "dp"),
            P(None, ("dp", "section")),
        ),
        check_vma=False,
    )
```

profile of v0, /device:TPU:1, one launch (start us, length us, event | category | flops | bytes accessed | tf_op | source)
XLA Modules:
  0.0 1298.5 jit_solution(6930351923376057090)
XLA Ops:
  11.7 81.5 %all-gather.3.cloned.1.call-done = bf16[1,1024,2048]{2,1,0:T(8,128)(2,1)} async-done(((bf16[1,1024,128]{2,1,0:T(8,128)(2,1)}), bf16[1,1024,2048]{2,1,0:T(8,128)(2,1)}) %all-gather.3.cloned.1.call-update) | async-done | bytes 4194320 | tf_op jit(solution)/shard_map/all_gather | solution.py:85
  93.2 78.8 %all-gather.5.cloned.1.call-done = bf16[1,2048,1024]{2,1,0:T(8,128)(2,1)} async-done(((bf16[1,128,1024]{2,1,0:T(8,128)(2,1)}), bf16[1,2048,1024]{2,1,0:T(8,128)(2,1)}) %all-gather.5.cloned.1.call-update) | async-done | bytes 4194320 | tf_op jit(solution)/shard_map/all_gather | solution.py:84
  179.6 172.7 %while.78 = (s32[]{:T(128)}, bf16[8,32,2048]{2,1,0:T(8,128)(2,1)}, bf16[8,32,2048]{2,1,0:T(8,128)(2,1)}, bf16[8,32,2048]{2,1,0:T(8,128)(2,1)}, bf16[8,32,1024]{2...) while((s32[]{:T(128)}, bf16[8,32,2048]{2,1,0:T(8,128)(2,1)}, ...), condition=%wide.region_7.8_spmd, body=%wide.region_0.7_spmd.sunk | while | flops 411418944 | bytes 34846988 | solution.py:151
  179.7 11.4 collective-permute-start
  196.8 4.4 collective-permute-done
  203.1 4.4 collective-permute-done
  247.4 5.1 collective-permute-done
  254.4 8.0 collective-permute-done
  264.3 8.0 collective-permute-done
  274.3 8.0 collective-permute-done
  284.2 50.3 %collective-permute-done = bf16[32,2048]{1,0:T(8,128)(2,1)S(1)} collective-permute-done((bf16[32,2048]{1,0:T(8,128)(2,1)S(1)}, bf16[32,2048]{1,0:T(8,128)(2,1)S(1)}, u32[]{:S(2)}, u32[]{:S(2)}) %collective-permute-start) | collective-permute-done | bytes 131104 | tf_op jit(solution)/shard_map/while/body/eval_jaxpr/ppermute | solution.py:15
  336.5 15.8 %collective-permute-done = bf16[32,2048]{1,0:T(8,128)(2,1)S(1)} collective-permute-done((bf16[32,2048]{1,0:T(8,128)(2,1)S(1)}, bf16[32,2048]{1,0:T(8,128)(2,1)S(1)}, u32[]{:S(2)}, u32[]{:S(2)}) %collective-permute-start) | collective-permute-done | bytes 131104 | tf_op jit(solution)/shard_map/while/body/eval_jaxpr/ppermute | solution.py:15
  352.3 250.0 %while.80 = (s32[]{:T(128)}, f32[32,2048]{1,0:T(8,128)S(1)}, bf16[8,32,2048]{2,1,0:T(8,128)(2,1)S(1)}, pred[]{:T(512)}, s32[]{:T(128)}, /*index=5*/f32[8,32,2048...) while((s32[]{:T(128)}, f32[32,2048]{1,0:T(8,128)S(1)}, ...), condition=%wide.region_9.10_spmd.clone, body=%wide.region_8.9_spmd.clone.sunk | while | flops 720906 | bytes 2621677 | solution.py:172
  353.3 13.4 %collective-permute-start.2 = (bf16[32,2048]{1,0:T(8,128)(2,1)S(1)}, bf16[32,2048]{1,0:T(8,128)(2,1)S(1)}, u32[]{:S(2)}, u32[]{:S(2)}) collective-permute-start(bf16[32,2048]{1,0:T(8,128)(2,1)S(1)} %fusion.126), channel_id=1, source_target_pairs={{15,0},{0,1},{1,2},{2,3},{3,4},{4,5},{5,6},{6,7},{7,8},{8,9},{9,10... | collective-permute-start | bytes 393224 | tf_op jit(solution)/shard_map/while/body/eval_jaxpr/ppermute | solution.py:21
  369.7 14.2 %collective-permute-start.2 = (bf16[32,2048]{1,0:T(8,128)(2,1)S(1)}, bf16[32,2048]{1,0:T(8,128)(2,1)S(1)}, u32[]{:S(2)}, u32[]{:S(2)}) collective-permute-start(bf16[32,2048]{1,0:T(8,128)(2,1)S(1)} %fusion.126), channel_id=1, source_target_pairs={{15,0},{0,1},{1,2},{2,3},{3,4},{4,5},{5,6},{6,7},{7,8},{8,9},{9,10... | collective-permute-start | bytes 393224 | tf_op jit(solution)/shard_map/while/body/eval_jaxpr/ppermute | solution.py:21
  385.0 21.1 %collective-permute-done.2 = bf16[32,2048]{1,0:T(8,128)(2,1)S(1)} collective-permute-done((bf16[32,2048]{1,0:T(8,128)(2,1)S(1)}, bf16[32,2048]{1,0:T(8,128)(2,1)S(1)}, u32[]{:S(2)}, u32[]{:S(2)}) %collective-permute-start.2) | collective-permute-done | bytes 131104 | tf_op jit(solution)/shard_map/while/body/eval_jaxpr/ppermute | solution.py:21
  408.2 6.9 collective-permute-done.2
  418.5 5.8 collective-permute-done.2
  425.4 8.3 collective-permute-start.2
  436.7 14.2 %collective-permute-start.2 = (bf16[32,2048]{1,0:T(8,128)(2,1)S(1)}, bf16[32,2048]{1,0:T(8,128)(2,1)S(1)}, u32[]{:S(2)}, u32[]{:S(2)}) collective-permute-start(bf16[32,2048]{1,0:T(8,128)(2,1)S(1)} %fusion.126), channel_id=1, source_target_pairs={{15,0},{0,1},{1,2},{2,3},{3,4},{4,5},{5,6},{6,7},{7,8},{8,9},{9,10... | collective-permute-start | bytes 393224 | tf_op jit(solution)/shard_map/while/body/eval_jaxpr/ppermute | solution.py:21
  466.1 6.1 collective-permute-start.2
  475.3 6.1 collective-permute-start.2
  484.4 6.1 collective-permute-start.2
  493.6 6.1 collective-permute-start.2
  502.7 6.1 collective-permute-start.2
  511.9 6.1 collective-permute-start.2
  521.0 6.1 collective-permute-start.2
  530.2 6.1 collective-permute-start.2
  539.3 6.1 collective-permute-start.2
  548.4 6.1 collective-permute-start.2
  557.6 6.1 collective-permute-start.2
  566.7 6.1 collective-permute-start.2
  575.9 6.1 collective-permute-start.2
  585.0 6.1 collective-permute-start.2
  594.2 6.1 collective-permute-start.2
  602.3 286.9 %while.79 = (s32[]{:T(128)}, bf16[8,32,2048]{2,1,0:T(8,128)(2,1)}, bf16[8,32,2048]{2,1,0:T(8,128)(2,1)}, bf16[8,32,2048]{2,1,0:T(8,128)(2,1)}, bf16[8,32,1024]{2...) while((s32[]{:T(128)}, bf16[8,32,2048]{2,1,0:T(8,128)(2,1)}, ...), condition=%wide.region_17.18_spmd, body=%wide.region_10.17_spmd.sunk | while | flops 410960192 | bytes 34182632 | solution.py:193
  602.4 5.1 collective-permute-start.1
  607.5 5.5 collective-permute-done.1
  615.0 7.8 collective-permute-done.1
  624.7 8.7 collective-permute-done.1
  635.4 7.8 collective-permute-done.1
  645.1 8.7 collective-permute-done.1
  655.7 67.8 %collective-permute-done.1 = bf16[32,2048]{1,0:T(8,128)(2,1)S(1)} collective-permute-done((bf16[32,2048]{1,0:T(8,128)(2,1)S(1)}, bf16[32,2048]{1,0:T(8,128)(2,1)S(1)}, u32[]{:S(2)}, u32[]{:S(2)}) %collective-permute-start.1) | collective-permute-done | bytes 131104 | tf_op jit(solution)/shard_map/while/body/eval_jaxpr/ppermute | solution.py:15
  723.5 10.0 conditional.5
  735.5 8.0 collective-permute-done.1
  743.4 10.0 conditional.5
  755.4 8.0 collective-permute-done.1
  763.4 10.1 conditional.5
  775.4 7.9 collective-permute-done.1
  783.4 10.1 conditional.5
  795.3 8.1 collective-permute-done.1
  803.4 10.1 conditional.5
  815.4 7.9 collective-permute-done.1
  823.3 10.1 conditional.5
  835.3 7.8 collective-permute-done.1
  843.1 10.0 conditional.5
  855.0 8.0 collective-permute-done.1
  863.0 10.0 conditional.5
  879.3 8.9 collective-permute-start.1
  892.0 4.6 bitcast_convert_fusion
  904.1 25.6 %all-reduce = bf16[2048]{0:T(1024)(128)(2,1)S(1)} all-reduce(bf16[2048]{0:T(1024)(128)(2,1)S(1)} %convert_element_type.234), channel_id=4, replica_groups=mesh['dp'=16,'section'=16] {'dp'}, use_global_device_ids=true, to_apply=%region_20.21.clone | all-reduce | flops 2048 | bytes 8192
  930.3 208.9 %all-reduce.4.cloned.1.call-done = f32[100,2048]{0,1:T(8,128)} async-done(((f32[100,2048]{0,1:T(8,128)}), f32[100,2048]{0,1:T(8,128)}) %all-reduce.4.cloned.1.call-update) | async-done | bytes 819216
  1140.4 71.7 %reduce-scatter.5.cloned.1.call-done = bf16[128,1024]{1,0:T(8,128)(2,1)} async-done(((bf16[2048,1024]{1,0:T(8,128)(2,1)}), bf16[128,1024]{1,0:T(8,128)(2,1)}) %reduce-scatter.5.cloned.1.call-update) | async-done | bytes 262160 | tf_op jit(solution)/shard_map/reduce_scatter | solution.py:221
  1214.0 78.0 %reduce-scatter.3.cloned.1.call-done = bf16[128,1024]{1,0:T(8,128)(2,1)} async-done(((bf16[2048,1024]{1,0:T(8,128)(2,1)}), bf16[128,1024]{1,0:T(8,128)(2,1)}) %reduce-scatter.3.cloned.1.call-update) | async-done | bytes 262160 | tf_op jit(solution)/shard_map/reduce_scatter | solution.py:218
  (400 shorter events, 266.0 us)
Async XLA Ops:
  7.2 86.0 %all-gather.3.cloned.1.call-start = ((), (), s32[]{:S(2)}) async-start(), calls=%async_computation.2 | async-start | bytes 4456448 | tf_op jit(solution)/shard_map/all_gather | solution.py:85
  7.9 164.1 %all-gather.5.cloned.1.call-start = ((), (), s32[]{:S(2)}) async-start(), calls=%async_computation.3 | async-start | bytes 4456448 | tf_op jit(solution)/shard_map/all_gather | solution.py:84
  8.6 1130.5 %all-reduce.4.cloned.1.call-start = ((), (), s32[]{:S(2)}) async-start(), calls=%async_computation.6 | async-start | bytes 2097152
  11.6 167.9 %copy-start.2 = (f32[1,2048]{1,0:T(1,128)S(1)}, f32[1,2048]{1,0:T(1,128)}, u32[]{:S(2)}) copy-start(f32[1,2048]{1,0:T(1,128)} %param.24) | copy-start | bytes 24580
  179.7 15.1 %collective-permute-start = (bf16[32,2048]{1,0:T(8,128)(2,1)S(1)}, bf16[32,2048]{1,0:T(8,128)(2,1)S(1)}, u32[]{:S(2)}, u32[]{:S(2)}) collective-permute-start(bf16[32,2048]{1,0:T(8,128)(2,1)S(1)} %get-tuple-element.1890), channel_id=1, source_target_pairs={{1,0},{2,1},{3,2},{4,3},{5,4},{6,5},{7,6},{8,7},{9,8},{10,9},{11,1... | collective-permute-start | bytes 393224 | tf_op jit(solution)/shard_map/while/body/eval_jaxpr/ppermute | solution.py:15
  194.8 6.3 collective-permute-start
  201.2 6.3 collective-permute-start
  207.5 6.3 collective-permute-start
  213.8 6.3 collective-permute-start
  220.1 6.3 collective-permute-start
  226.5 6.3 collective-permute-start
  232.8 6.3 collective-permute-start
  239.1 6.3 collective-permute-start
  245.4 7.0 collective-permute-start
  252.5 9.9 collective-permute-start
  262.4 9.9 collective-permute-start
  272.4 9.9 collective-permute-start
  282.3 52.2 %collective-permute-start = (bf16[32,2048]{1,0:T(8,128)(2,1)S(1)}, bf16[32,2048]{1,0:T(8,128)(2,1)S(1)}, u32[]{:S(2)}, u32[]{:S(2)}) collective-permute-start(bf16[32,2048]{1,0:T(8,128)(2,1)S(1)} %get-tuple-element.1890), channel_id=1, source_target_pairs={{1,0},{2,1},{3,2},{4,3},{5,4},{6,5},{7,6},{8,7},{9,8},{10,9},{11,1... | collective-permute-start | bytes 393224 | tf_op jit(solution)/shard_map/while/body/eval_jaxpr/ppermute | solution.py:15
  334.5 17.8 %collective-permute-start = (bf16[32,2048]{1,0:T(8,128)(2,1)S(1)}, bf16[32,2048]{1,0:T(8,128)(2,1)S(1)}, u32[]{:S(2)}, u32[]{:S(2)}) collective-permute-start(bf16[32,2048]{1,0:T(8,128)(2,1)S(1)} %get-tuple-element.1890), channel_id=1, source_target_pairs={{1,0},{2,1},{3,2},{4,3},{5,4},{6,5},{7,6},{8,7},{9,8},{10,9},{11,1... | collective-permute-start | bytes 393224 | tf_op jit(solution)/shard_map/while/body/eval_jaxpr/ppermute | solution.py:15
  353.3 15.3 %collective-permute-start.2 = (bf16[32,2048]{1,0:T(8,128)(2,1)S(1)}, bf16[32,2048]{1,0:T(8,128)(2,1)S(1)}, u32[]{:S(2)}, u32[]{:S(2)}) collective-permute-start(bf16[32,2048]{1,0:T(8,128)(2,1)S(1)} %fusion.126), channel_id=1, source_target_pairs={{15,0},{0,1},{1,2},{2,3},{3,4},{4,5},{5,6},{6,7},{7,8},{8,9},{9,10... | collective-permute-start | bytes 393224 | tf_op jit(solution)/shard_map/while/body/eval_jaxpr/ppermute | solution.py:21
  369.7 36.4 %collective-permute-start.2 = (bf16[32,2048]{1,0:T(8,128)(2,1)S(1)}, bf16[32,2048]{1,0:T(8,128)(2,1)S(1)}, u32[]{:S(2)}, u32[]{:S(2)}) collective-permute-start(bf16[32,2048]{1,0:T(8,128)(2,1)S(1)} %fusion.126), channel_id=1, source_target_pairs={{15,0},{0,1},{1,2},{2,3},{3,4},{4,5},{5,6},{6,7},{7,8},{8,9},{9,10... | collective-permute-start | bytes 393224 | tf_op jit(solution)/shard_map/while/body/eval_jaxpr/ppermute | solution.py:21
  407.1 8.1 collective-permute-start.2
  416.2 8.1 collective-permute-start.2
  425.4 10.3 collective-permute-start.2
  436.7 16.2 %collective-permute-start.2 = (bf16[32,2048]{1,0:T(8,128)(2,1)S(1)}, bf16[32,2048]{1,0:T(8,128)(2,1)S(1)}, u32[]{:S(2)}, u32[]{:S(2)}) collective-permute-start(bf16[32,2048]{1,0:T(8,128)(2,1)S(1)} %fusion.126), channel_id=1, source_target_pairs={{15,0},{0,1},{1,2},{2,3},{3,4},{4,5},{5,6},{6,7},{7,8},{8,9},{9,10... | collective-permute-start | bytes 393224 | tf_op jit(solution)/shard_map/while/body/eval_jaxpr/ppermute | solution.py:21
  453.9 4.5 collective-permute-start.2
  459.4 5.6 collective-permute-start.2
  466.1 8.1 collective-permute-start.2
  475.3 8.1 collective-permute-start.2
  484.4 8.1 collective-permute-start.2
  493.6 8.1 collective-permute-start.2
  502.7 8.1 collective-permute-start.2
  511.9 8.1 collective-permute-start.2
  521.0 8.1 collective-permute-start.2
  530.2 8.1 collective-permute-start.2
  539.3 8.1 collective-permute-start.2
  548.4 8.1 collective-permute-start.2
  557.6 8.1 collective-permute-start.2
  566.7 8.1 collective-permute-start.2
  575.9 8.1 collective-permute-start.2
  585.0 8.1 collective-permute-start.2
  594.2 8.1 collective-permute-start.2
  602.4 10.6 collective-permute-start.1
  613.0 9.7 collective-permute-start.1
  622.8 10.6 collective-permute-start.1
  633.4 9.7 collective-permute-start.1
  643.2 10.6 collective-permute-start.1
  653.8 69.7 %collective-permute-start.1 = (bf16[32,2048]{1,0:T(8,128)(2,1)S(1)}, bf16[32,2048]{1,0:T(8,128)(2,1)S(1)}, u32[]{:S(2)}, u32[]{:S(2)}) collective-permute-start(bf16[32,2048]{1,0:T(8,128)(2,1)S(1)} %get-tuple-element.1917), channel_id=1, source_target_pairs={{1,0},{2,1},{3,2},{4,3},{5,4},{6,5},{7,6},{8,7},{9,8},{10,9},{11,1... | collective-permute-start | bytes 393224 | tf_op jit(solution)/shard_map/while/body/eval_jaxpr/ppermute | solution.py:15
  723.5 4.9 copy-start.1
  733.6 9.9 collective-permute-start.1
  743.4 4.9 copy-start.1
  753.5 10.0 collective-permute-start.1
  763.4 4.9 copy-start.1
  773.5 9.9 collective-permute-start.1
  793.4 10.0 collective-permute-start.1
  803.4 4.9 copy-start.1
  813.5 9.8 collective-permute-start.1
  823.3 4.9 copy-start.1
  833.4 9.7 collective-permute-start.1
  853.1 9.9 collective-permute-start.1
  873.0 6.3 collective-permute-start.1
  879.3 9.8 collective-permute-start.1
  891.9 320.3 %reduce-scatter.5.cloned.1.call-start = ((), (), s32[]{:S(2)}) async-start(), calls=%async_computation.5 | async-start | bytes 4456448 | tf_op jit(solution)/shard_map/reduce_scatter | solution.py:221
  896.6 395.3 %reduce-scatter.3.cloned.1.call-start = ((), (), s32[]{:S(2)}) async-start(), calls=%async_computation.4 | async-start | bytes 4456448 | tf_op jit(solution)/shard_map/reduce_scatter | solution.py:218
  (7 other events, 19.9 us)
Sparse Core Ops, SparseCore 0:
  9.7 83.4 all-gather.2
  94.9 77.0 all-gather.4
  892.1 247.0 all-reduce.3
  1141.7 70.3 reduce-scatter.4
  1215.3 76.5 reduce-scatter.2
where the time goes:
time: 1310 us; the launch traced here: 1300 us
  waiting for transfers between devices  873 us (67%)
  starting transfers between devices  227 us (17%)
  other arithmetic  68.6 us (5%)
  matrix products  64.7 us (5%)
  blocking collectives  25.6 us (2%)
  local copies, waits for them, and re-layouts  22.4 us (2%)
  between operations  14.6 us (1%)
    ppermute x30, waiting for transfers between devices, shifted(): return lax.ppermute(block, axis, route)  301 us
    unnamed x6, waiting for transfers between devices  210 us
    ppermute x23, starting transfers between devices, passed_along(): return lax.ppermute(block, axis, route)  150 us
    all_gather x1, waiting for transfers between devices, body(): lax.all_gather(out_weight, 'dp', axis=2, tiled=True)  81.5 us
    all_gather x1, waiting for transfers between devices, body(): lax.all_gather(value_weight, 'dp', axis=1, tiled=True)  78.8 us
    reduce_scatter x1, waiting for transfers between devices, body(): lax.psum_scatter(value_term.astype(jnp.bfloat16), 'dp', scatter_dimension...  78 us
    ppermute x30, starting transfers between devices, shifted(): return lax.ppermute(block, axis, route)  77.1 us
    reduce_scatter x1, waiting for transfers between devices, body(): lax.psum_scatter(output_term.astype(jnp.bfloat16), 'dp', scatter_dimensio...  71.7 us
  transfers between devices with their start and end apart: 58, of which 58 were waited for; matrix products, arithmetic and copies ran while one was open for 3% of the time, Pallas kernels for 0%

commit v1 on v0

v1 whole, which is shorter than its diff:
```python
import jax
import jax.numpy as jnp
from jax import lax
from jax.sharding import PartitionSpec as P

SENT = 100
GROUP = 2
EPSILON = 1e-06


def chain_pairs(count, half):
    down = [(s, s - 2) for s in range(half + 1, count)]
    return down + [(s, s - 1) for s in range(1, half)]


def relay_pairs(count, half):
    return [(s, s + 1) for s in range(half, count - 2, 2)]


def chain_lag(section, count, half):
    decoder = (count - 1 - section) // 2
    encoder = half // 2 + (half - 1 - section)
    return jnp.where(section >= half, decoder, encoder)


def body(
    section_inputs,
    enc_output,
    attention_probs,
    value_weight,
    out_weight,
    norm_gain,
    top_grad,
    enc_sentinel,
    dec_sentinel,
):
    count = lax.axis_size("section")
    dp_count = lax.axis_size("dp")
    half = count // 2
    section = lax.axis_index("section")
    in_decoder = section >= half
    is_cross = jnp.logical_and(in_decoder, (section - half) % 2 == 1)
    is_top = section >= count - 2
    gathered = lax.all_gather(
        jnp.concatenate([value_weight[0], out_weight[0].T], axis=1), "dp", axis=0, tiled=True
    )
    inner = value_weight.shape[2]
    w_value = gathered[:, :inner]
    w_out = gathered[:, inner:]
    gain_row = norm_gain[0]
    micro, length = enc_sentinel.shape
    width = section_inputs.shape[2]
    heads = attention_probs.shape[2]
    rows = micro * length
    slots = micro // GROUP
    block = GROUP * length

    source = jnp.where(is_cross, enc_output, section_inputs[0])
    widened = source.astype(jnp.float32)
    inverse = lax.rsqrt(jnp.mean(widened * widened, axis=-1, keepdims=True) + EPSILON)
    normed = (widened * inverse * gain_row).astype(jnp.bfloat16)
    values = jnp.dot(normed, w_value, preferred_element_type=jnp.float32).astype(jnp.bfloat16)
    probs = attention_probs[0]
    source_slots = source.reshape(slots, block, width)
    inverse_slots = inverse.reshape(slots, block, 1)
    probs_slots = probs.reshape(slots, GROUP, heads, length, length)
    top_slots = top_grad.reshape(slots, block, width)
    lag = chain_lag(section, count, half)

    def pick(table, slot):
        return lax.dynamic_index_in_dim(table, slot, 0, keepdims=False)

    in_store = jnp.zeros((slots + 1, block, width), jnp.bfloat16)
    out_store = jnp.zeros((slots + 1, block, width), jnp.bfloat16)
    ctx_store = jnp.zeros((slots + 1, block, inner), jnp.bfloat16)
    vgrad_store = jnp.zeros((slots + 1, block, inner), jnp.bfloat16)
    gain_total = jnp.zeros((width,), jnp.float32)
    zeros = jnp.zeros((block, width), jnp.bfloat16)
    send = zeros
    for step in range(slots + half // 2 + half - 1):
        raw = step - lag
        active = jnp.logical_and(raw >= 0, raw < slots)
        slot = jnp.clip(raw, 0, slots - 1)
        keep = jnp.where(active, slot, slots)
        if step > 0:
            arrived = lax.ppermute(send, "section", chain_pairs(count, half))
            relayed = lax.ppermute(arrived, "section", relay_pairs(count, half))
        else:
            arrived = zeros
            relayed = zeros
        out_grad = jnp.where(is_top, pick(top_slots, slot), jnp.where(is_cross, relayed, arrived))
        ctx_grad = lax.dot_general(
            out_grad, w_out, (((1,), (0,)), ((), ())), preferred_element_type=jnp.float32
        ).astype(jnp.bfloat16)
        value_grad = jnp.einsum(
            "bhqk,bqhd->bkhd",
            pick(probs_slots, slot),
            ctx_grad.reshape(GROUP, length, heads, -1),
            preferred_element_type=jnp.float32,
        )
        value_grad = value_grad.astype(jnp.bfloat16).reshape(block, inner)
        normed_grad = lax.dot_general(
            value_grad, w_value, (((1,), (1,)), ((), ())), preferred_element_type=jnp.float32
        )
        scale = pick(inverse_slots, slot)
        unit = pick(source_slots, slot).astype(jnp.float32) * scale
        scaled = normed_grad * gain_row
        source_grad = scale * (scaled - unit * jnp.mean(scaled * unit, axis=-1, keepdims=True))
        gain_total = gain_total + jnp.where(active, jnp.sum(normed_grad * unit, axis=0), 0.0)
        widened_out = out_grad.astype(jnp.float32)
        in_grad = jnp.where(is_cross, widened_out, widened_out + source_grad).astype(jnp.bfloat16)
        running = jnp.where(section == count - 1, 0.0, arrived.astype(jnp.float32)) + source_grad
        send = jnp.where(is_cross, running.astype(jnp.bfloat16), in_grad)

        def put(store, piece):
            return lax.dynamic_update_index_in_dim(store, piece, keep, 0)

        in_store = put(in_store, in_grad)
        out_store = put(out_store, out_grad)
        ctx_store = put(ctx_store, ctx_grad)
        vgrad_store = put(vgrad_store, value_grad)

    in_rows = in_store[:slots].reshape(rows, width)
    out_rows = out_store[:slots].reshape(rows, width)
    value_rows = vgrad_store[:slots].reshape(rows, inner)
    head_grads = ctx_store[:slots].reshape(micro, length, heads, -1)
    head_values = values.reshape(micro, length, heads, -1)
    context = jnp.einsum(
        "bhqk,bkhd->bqhd", probs, head_values, preferred_element_type=jnp.float32
    )
    context = context.astype(jnp.bfloat16).reshape(rows, inner)
    prob_grad = jnp.einsum(
        "bqhd,bkhd->bhqk", head_grads, head_values, preferred_element_type=jnp.float32
    )
    prob_wide = probs.astype(jnp.float32)
    score_grad = (
        prob_wide * (prob_grad - jnp.sum(prob_grad * prob_wide, axis=-1, keepdims=True))
    ).astype(jnp.bfloat16)
    chosen = jnp.where(
        section == 0, enc_sentinel, jnp.where(section == half, dec_sentinel, SENT)
    )
    table = (chosen.reshape(1, -1) == jnp.arange(SENT, dtype=jnp.int32)[:, None]).astype(
        jnp.bfloat16
    )
    sentinel_term = jnp.dot(table, in_rows, preferred_element_type=jnp.float32)
    small = jnp.concatenate([sentinel_term, gain_total[None], jnp.zeros((3, width))], axis=0)
    small_rows = small.shape[0]
    small = small.astype(jnp.bfloat16).reshape(small_rows, dp_count, -1).transpose(1, 0, 2)
    piece = width // dp_count
    small = small.reshape(dp_count, -1, inner)
    value_term = jnp.einsum("td,ti->di", normed, value_rows, preferred_element_type=jnp.float32)
    output_term = jnp.einsum("td,ti->di", out_rows, context, preferred_element_type=jnp.float32)
    payload = jnp.concatenate(
        [
            value_term.astype(jnp.bfloat16).reshape(dp_count, piece, inner),
            output_term.astype(jnp.bfloat16).reshape(dp_count, piece, inner),
            small,
            jnp.zeros((dp_count, -small.shape[1] % 16, inner), jnp.bfloat16),
        ],
        axis=1,
    )
    summed = lax.psum_scatter(payload, "dp", scatter_dimension=0, tiled=True)[0]
    small_sum = summed[2 * piece : 2 * piece + small.shape[1]].reshape(small_rows, piece)
    small_sum = small_sum.astype(jnp.float32)
    sentinel_grad = lax.psum_scatter(
        small_sum[:SENT], "section", scatter_dimension=1, tiled=True
    )
    return (
        in_rows[None],
        score_grad[None],
        summed[:piece][None],
        summed[piece : 2 * piece].T[None],
        small_sum[SENT][None],
        sentinel_grad,
    )


def solution(mesh):
    placed = (
        P("section", "dp", None),
        P("dp", None),
        P("section", "dp", None, None, None),
        P("section", "dp", None),
        P("section", None, "dp"),
        P("section", None),
        P("dp", None),
        P("dp", None),
        P("dp", None),
    )
    return jax.shard_map(
        body,
        mesh=mesh,
        in_specs=placed,
        out_specs=(
            P("section", "dp", None),
            P("section", "dp", None, None, None),
            P("section", "dp", None),
            P("section", None, "dp"),
            P("section", "dp"),
            P(None, ("dp", "section")),
        ),
        check_vma=False,
    )
```

time: 1310 us -> 728 us (0.56)
  waiting for transfers between devices: 873 us -> 341 us
  starting transfers between devices: 227 us -> 53.3 us
  matrix products: 64.7 us -> 130 us
  blocking collectives: 25.6 us -> 63.9 us
  local copies, waits for them, and re-layouts: 22.4 us -> 59.7 us
  other arithmetic: 68.6 us -> 49.5 us
    ppermute x53 -> x28, waiting for transfers between devices: 353 us -> 80.8 us  [the longest x14 80.8 us: body(): arrived = lax.ppermute(send, 'section', chain_pairs(count, half))]
    unnamed x6 -> x2, waiting for transfers between devices: 210 us -> 0.03 us
    ppermute x53 -> x28, starting transfers between devices: 227 us -> 53.2 us  [the longest x14 33.6 us: body(): arrived = lax.ppermute(send, 'section', chain_pairs(count, half))]
    dot_general x51, matrix products: 64.7 us -> 130 us  [the longest x15 62.6 us: body(): lax.dot_general(out_grad, w_out, (((1,), (0,)), ((), ())), preferred_elem...]
    all_gather x2 -> x1, waiting for transfers between devices: 160 us -> 120 us  [body(): lax.all_gather(jnp.concatenate([value_weight[0], out_weight[0].T], axis=1...]
    unnamed x1, blocking collectives: 25.6 us -> 63.9 us
    convert_element_type x47 -> x1, other arithmetic: 23.5 us -> 0.76 us  [body(): small_sum = small_sum.astype(jnp.float32)]
    broadcast_in_dim x42 -> x17, local copies, waits for them, and re-layouts: 1.72 us -> 15.9 us  [the longest x15 14.1 us: put(): return lax.dynamic_update_index_in_dim(store, piece, keep, 0)]
  transfers between devices with their start and end apart: 58 -> 30, of which waited for: 58 -> 16; matrix products, arithmetic and copies ran while one was open for 3% -> 6% of each run, Pallas kernels for 0% -> 0%
where the time goes in v1:
time: 728 us; the launch traced here: 714 us
  waiting for transfers between devices  341 us (47%)
  matrix products  130 us (18%)
  blocking collectives  63.9 us (9%)
  local copies, waits for them, and re-layouts  59.7 us (8%)
  starting transfers between devices  53.3 us (7%)
  other arithmetic  49.5 us (7%)
  between operations  17.1 us (2%)
    reduce_scatter x1, waiting for transfers between devices, body(): summed = lax.psum_scatter(payload, 'dp', scatter_dimension=0, tiled=True)[0]  140 us
    all_gather x1, waiting for transfers between devices, body(): lax.all_gather(jnp.concatenate([value_weight[0], out_weight[0].T], axis=1...  120 us
    ppermute x14, waiting for transfers between devices, body(): arrived = lax.ppermute(send, 'section', chain_pairs(count, half))  80.8 us
    unnamed x1, blocking collectives  63.9 us
    dot_general x15, matrix products, body(): lax.dot_general(out_grad, w_out, (((1,), (0,)), ((), ())), preferred_elem...  62.6 us
    dot_general x15, matrix products, body(): lax.dot_general(value_grad, w_value, (((1,), (1,)), ((), ())), preferred_...  55.7 us
    ppermute x14, starting transfers between devices, body(): arrived = lax.ppermute(send, 'section', chain_pairs(count, half))  33.6 us
    dynamic_update_slice x29, other arithmetic, put(): return lax.dynamic_update_index_in_dim(store, piece, keep, 0)  31.2 us
  transfers between devices with their start and end apart: 30, of which 16 were waited for; matrix products, arithmetic and copies ran while one was open for 6% of the time, Pallas kernels for 0%

profile of v1, /device:TPU:1, one launch (start us, length us, event | category | flops | bytes accessed | tf_op | source)
XLA Modules:
  0.0 713.9 jit_solution(13294302353149168123)
XLA Ops:
  13.0 120.1 %all-gather.2.cloned.1.call-done = bf16[2048,2048]{0,1:T(8,128)(2,1)} async-done(((bf16[128,2048]{0,1:T(8,128)(2,1)}), bf16[2048,2048]{0,1:T(8,128)(2,1)}) %all-gather.2.cloned.1.call-update) | async-done | bytes 8388624 | tf_op jit(solution)/shard_map/all_gather | solution.py:44
  134.0 4.2 bitcast_dynamic-update-slice_fusion.42
  138.6 3.7 fusion.147
  143.3 8.8 %collective-permute-start = (bf16[64,2048]{1,0:T(8,128)(2,1)S(1)}, bf16[64,2048]{1,0:T(8,128)(2,1)S(1)}, u32[]{:S(2)}, u32[]{:S(2)}) collective-permute-start(bf16[64,2048]{1,0:T(8,128)(2,1)S(1)} %convert_select_fusion), channel_id=1, source_target_pairs={{9,7},{10,8},{11,9},{12,10},{13,11},{14,12},{15,13},{1,0},{2,1},{3... | collective-permute-start | bytes 786440 | tf_op jit(solution)/shard_map/ppermute | solution.py:86
  152.2 4.0 collective-permute-done
  159.6 4.2 bitcast_dynamic-update-slice_fusion.41
  164.2 3.7 fusion.140
  169.0 1.9 collective-permute-start.2
  171.0 5.8 collective-permute-done.2
  178.9 4.3 bitcast_dynamic-update-slice_fusion.40
  183.6 3.8 fusion.133
  188.2 1.9 collective-permute-start.4
  190.1 5.8 collective-permute-done.4
  198.1 4.3 bitcast_dynamic-update-slice_fusion.39
  202.7 3.8 fusion.126
  207.3 1.9 collective-permute-start.6
  209.2 5.8 collective-permute-done.6
  217.6 4.3 bitcast_dynamic-update-slice_fusion.38
  222.3 3.8 fusion.119
  226.9 1.9 collective-permute-start.8
  228.8 5.8 collective-permute-done.8
  236.7 4.3 bitcast_dynamic-update-slice_fusion.37
  241.4 3.8 fusion.112
  246.0 1.9 collective-permute-start.10
  247.9 5.8 collective-permute-done.10
  255.9 4.3 bitcast_dynamic-update-slice_fusion.36
  260.5 3.7 fusion.105
  267.0 5.8 collective-permute-done.12
  275.0 4.3 bitcast_dynamic-update-slice_fusion.35
  279.7 3.7 fusion.98
  286.2 5.8 collective-permute-done.14
  294.3 4.3 bitcast_dynamic-update-slice_fusion.34
  299.0 3.7 fusion.91
  303.5 1.9 collective-permute-start.16
  305.4 5.8 collective-permute-done.16
  313.4 4.3 bitcast_dynamic-update-slice_fusion.33
  318.1 3.8 fusion.84
  324.6 5.8 collective-permute-done.18
  332.6 4.3 bitcast_dynamic-update-slice_fusion.32
  337.2 3.7 fusion.77
  343.7 6.4 collective-permute-done.20
  354.2 4.3 bitcast_dynamic-update-slice_fusion.31
  358.8 3.8 fusion.70
  363.4 1.9 collective-permute-start.22
  365.3 3.5 fusion.8
  368.9 7.3 %collective-permute-done.22 = bf16[64,2048]{1,0:T(8,128)(2,1)} collective-permute-done((bf16[64,2048]{1,0:T(8,128)(2,1)S(1)}, bf16[64,2048]{1,0:T(8,128)(2,1)}, u32[]{:S(2)}, u32[]{:S(2)}) %collective-permute-start.22) | collective-permute-done | bytes 262176 | tf_op jit(solution)/shard_map/ppermute | solution.py:86
  379.6 2.0 copy.425
  389.1 4.3 bitcast_dynamic-update-slice_fusion.30
  393.8 3.8 fusion.63
  397.6 2.1 fusion.167
  399.7 1.9 collective-permute-start.24
  407.1 5.5 collective-permute-done.24
  421.3 4.3 bitcast_dynamic-update-slice_fusion.29
  425.9 3.7 fusion.56
  429.7 2.1 fusion.168
  431.8 1.9 collective-permute-start.26
  439.3 5.7 collective-permute-done.26
  451.9 2.3 bitcast_dynamic-update-slice_fusion
  469.3 2.0 bitcast_dynamic-update-slice_fusion.28
  471.9 3.3 fusion.49
  476.2 2.3 slice.52
  488.5 5.1 maximum_maximum_fusion
  498.4 139.6 %reduce-scatter.3.cloned.1.call-done = bf16[1,272,1024]{2,1,0:T(8,128)(2,1)} async-done(((bf16[16,272,1024]{2,1,0:T(8,128)(2,1)}), bf16[1,272,1024]{2,1,0:T(8,128)(2,1)}) %reduce-scatter.3.cloned.1.call-update) | async-done | bytes 557072 | tf_op jit(solution)/shard_map/reduce_scatter | solution.py:162
  641.9 63.9 %all-reduce = f32[100,128]{1,0:T(8,128)S(1)} all-reduce(f32[100,128]{1,0:T(8,128)S(1)} %bitcast.821), channel_id=3, replica_groups=mesh['dp'=16,'section'=16] {'section'}, use_global_device_ids=true, to_apply=%region_33.34.clone | all-reduce | flops 12800 | bytes 102400
  (487 shorter events, 128.6 us)
Async XLA Ops:
  7.2 126.9 %copy-start = (bf16[256,2048]{1,0:T(8,128)(2,1)S(1)}, bf16[256,2048]{1,0:T(8,128)(2,1)}, u32[]{:S(2)}) copy-start(bf16[256,2048]{1,0:T(8,128)(2,1)} %param.15) | copy-start | bytes 3145732
  7.2 125.9 %all-gather.2.cloned.1.call-start = ((), (), s32[]{:S(2)}) async-start(), calls=%async_computation.1 | async-start | bytes 8912896 | tf_op jit(solution)/shard_map/all_gather | solution.py:44
  10.2 627.7 %reduce-scatter.3.cloned.1.call-start = ((), (), s32[]{:S(2)}) async-start(), calls=%async_computation.2 | async-start | bytes 9469952 | tf_op jit(solution)/shard_map/reduce_scatter | solution.py:162
  10.3 127.9 %copy-start.1 = (bf16[1,8,8,32,32]{4,3,2,1,0:T(8,128)(2,1)S(1)}, bf16[1,8,8,32,32]{4,3,2,1,0:T(8,128)(2,1)}, u32[]{:S(2)}) copy-start(bf16[1,8,8,32,32]{4,3,2,1,0:T(8,128)(2,1)} %param.11) | copy-start | bytes 393220
  12.1 126.4 %copy-start.2 = (f32[1,2048]{1,0:T(1,128)S(1)}, f32[1,2048]{1,0:T(1,128)}, u32[]{:S(2)}) copy-start(f32[1,2048]{1,0:T(1,128)} %param.14) | copy-start | bytes 24580
  13.0 129.3 %copy-start.110 = (f32[64]{0:T(128)}, f32[64]{0:T(128)S(1)}, u32[]{:S(2)}) copy-start(f32[64]{0:T(128)S(1)} %get-tuple-element.119) | copy-start | bytes 772
  142.3 16.5 %copy-start.137 = (f32[64]{0:T(128)}, f32[64]{0:T(128)S(1)}, u32[]{:S(2)}) copy-start(f32[64]{0:T(128)S(1)} %broadcast_multiply_fusion.14) | copy-start | bytes 772
  143.3 12.8 %collective-permute-start = (bf16[64,2048]{1,0:T(8,128)(2,1)S(1)}, bf16[64,2048]{1,0:T(8,128)(2,1)S(1)}, u32[]{:S(2)}, u32[]{:S(2)}) collective-permute-start(bf16[64,2048]{1,0:T(8,128)(2,1)S(1)} %convert_select_fusion), channel_id=1, source_target_pairs={{9,7},{10,8},{11,9},{12,10},{13,11},{14,12},{15,13},{1,0},{2,1},{3... | collective-permute-start | bytes 786440 | tf_op jit(solution)/shard_map/ppermute | solution.py:86
  156.2 2.7 collective-permute-start.1
  164.2 14.7 %copy-start.58 = (bf16[2,32,8,128]{3,2,1,0:T(8,128)(2,1)}, bf16[2,32,8,128]{3,2,1,0:T(8,128)(2,1)S(1)}, u32[]{:S(2)}) copy-start(bf16[2,32,8,128]{3,2,1,0:T(8,128)(2,1)S(1)} %copy.365) | copy-start | bytes 393220
  168.0 11.0 %copy-start.113 = (f32[64]{0:T(128)}, f32[64]{0:T(128)S(1)}, u32[]{:S(2)}) copy-start(f32[64]{0:T(128)S(1)} %broadcast_multiply_fusion.13) | copy-start | bytes 772
  169.0 7.7 %collective-permute-start.2 = (bf16[64,2048]{1,0:T(8,128)(2,1)S(1)}, bf16[64,2048]{1,0:T(8,128)(2,1)S(1)}, u32[]{:S(2)}, u32[]{:S(2)}) collective-permute-start(bf16[64,2048]{1,0:T(8,128)(2,1)S(1)} %fusion.156), channel_id=1, source_target_pairs={{9,7},{10,8},{11,9},{12,10},{13,11},{14,12},{15,13},{1,0},{2,1},{3... | collective-permute-start | bytes 786440 | tf_op jit(solution)/shard_map/ppermute | solution.py:86
  176.7 1.4 collective-permute-start.3
  183.6 14.5 %copy-start.59 = (bf16[2,32,8,128]{3,2,1,0:T(8,128)(2,1)}, bf16[2,32,8,128]{3,2,1,0:T(8,128)(2,1)S(1)}, u32[]{:S(2)}) copy-start(bf16[2,32,8,128]{3,2,1,0:T(8,128)(2,1)S(1)} %copy.368) | copy-start | bytes 393220
  187.4 10.7 %copy-start.114 = (f32[64]{0:T(128)}, f32[64]{0:T(128)S(1)}, u32[]{:S(2)}) copy-start(f32[64]{0:T(128)S(1)} %broadcast_multiply_fusion.12) | copy-start | bytes 772
  188.2 7.7 %collective-permute-start.4 = (bf16[64,2048]{1,0:T(8,128)(2,1)S(1)}, bf16[64,2048]{1,0:T(8,128)(2,1)S(1)}, u32[]{:S(2)}, u32[]{:S(2)}) collective-permute-start(bf16[64,2048]{1,0:T(8,128)(2,1)S(1)} %fusion.157), channel_id=1, source_target_pairs={{9,7},{10,8},{11,9},{12,10},{13,11},{14,12},{15,13},{1,0},{2,1},{3... | collective-permute-start | bytes 786440 | tf_op jit(solution)/shard_map/ppermute | solution.py:86
  195.8 1.4 collective-permute-start.5
  202.7 14.9 %copy-start.60 = (bf16[2,32,8,128]{3,2,1,0:T(8,128)(2,1)}, bf16[2,32,8,128]{3,2,1,0:T(8,128)(2,1)S(1)}, u32[]{:S(2)}) copy-start(bf16[2,32,8,128]{3,2,1,0:T(8,128)(2,1)S(1)} %copy.371) | copy-start | bytes 393220
  206.5 11.1 %copy-start.115 = (f32[64]{0:T(128)}, f32[64]{0:T(128)S(1)}, u32[]{:S(2)}) copy-start(f32[64]{0:T(128)S(1)} %broadcast_multiply_fusion.11) | copy-start | bytes 772
  207.3 7.7 %collective-permute-start.6 = (bf16[64,2048]{1,0:T(8,128)(2,1)S(1)}, bf16[64,2048]{1,0:T(8,128)(2,1)S(1)}, u32[]{:S(2)}, u32[]{:S(2)}) collective-permute-start(bf16[64,2048]{1,0:T(8,128)(2,1)S(1)} %fusion.158), channel_id=1, source_target_pairs={{9,7},{10,8},{11,9},{12,10},{13,11},{14,12},{15,13},{1,0},{2,1},{3... | collective-permute-start | bytes 786440 | tf_op jit(solution)/shard_map/ppermute | solution.py:86
  215.0 1.8 collective-permute-start.7
  222.3 14.4 %copy-start.62 = (bf16[2,32,8,128]{3,2,1,0:T(8,128)(2,1)}, bf16[2,32,8,128]{3,2,1,0:T(8,128)(2,1)S(1)}, u32[]{:S(2)}) copy-start(bf16[2,32,8,128]{3,2,1,0:T(8,128)(2,1)S(1)} %copy.374) | copy-start | bytes 393220
  226.1 10.7 %copy-start.116 = (f32[64]{0:T(128)}, f32[64]{0:T(128)S(1)}, u32[]{:S(2)}) copy-start(f32[64]{0:T(128)S(1)} %broadcast_multiply_fusion.10) | copy-start | bytes 772
  226.9 7.7 %collective-permute-start.8 = (bf16[64,2048]{1,0:T(8,128)(2,1)S(1)}, bf16[64,2048]{1,0:T(8,128)(2,1)S(1)}, u32[]{:S(2)}, u32[]{:S(2)}) collective-permute-start(bf16[64,2048]{1,0:T(8,128)(2,1)S(1)} %fusion.159), channel_id=1, source_target_pairs={{9,7},{10,8},{11,9},{12,10},{13,11},{14,12},{15,13},{1,0},{2,1},{3... | collective-permute-start | bytes 786440 | tf_op jit(solution)/shard_map/ppermute | solution.py:86
  234.5 1.4 collective-permute-start.9
  241.4 14.4 %copy-start.63 = (bf16[2,32,8,128]{3,2,1,0:T(8,128)(2,1)}, bf16[2,32,8,128]{3,2,1,0:T(8,128)(2,1)S(1)}, u32[]{:S(2)}) copy-start(bf16[2,32,8,128]{3,2,1,0:T(8,128)(2,1)S(1)} %copy.377) | copy-start | bytes 393220
  245.2 10.7 %copy-start.118 = (f32[64]{0:T(128)}, f32[64]{0:T(128)S(1)}, u32[]{:S(2)}) copy-start(f32[64]{0:T(128)S(1)} %broadcast_multiply_fusion.9) | copy-start | bytes 772
  246.0 7.7 %collective-permute-start.10 = (bf16[64,2048]{1,0:T(8,128)(2,1)S(1)}, bf16[64,2048]{1,0:T(8,128)(2,1)S(1)}, u32[]{:S(2)}, u32[]{:S(2)}) collective-permute-start(bf16[64,2048]{1,0:T(8,128)(2,1)S(1)} %fusion.160), channel_id=1, source_target_pairs={{9,7},{10,8},{11,9},{12,10},{13,11},{14,12},{15,13},{1,0},{2,1},{3... | collective-permute-start | bytes 786440 | tf_op jit(solution)/shard_map/ppermute | solution.py:86
  253.7 1.4 collective-permute-start.11
  260.5 14.4 %copy-start.64 = (bf16[2,32,8,128]{3,2,1,0:T(8,128)(2,1)}, bf16[2,32,8,128]{3,2,1,0:T(8,128)(2,1)S(1)}, u32[]{:S(2)}) copy-start(bf16[2,32,8,128]{3,2,1,0:T(8,128)(2,1)S(1)} %copy.380) | copy-start | bytes 393220
  264.3 10.7 %copy-start.120 = (f32[64]{0:T(128)}, f32[64]{0:T(128)S(1)}, u32[]{:S(2)}) copy-start(f32[64]{0:T(128)S(1)} %broadcast_multiply_fusion.8) | copy-start | bytes 772
  265.1 7.7 %collective-permute-start.12 = (bf16[64,2048]{1,0:T(8,128)(2,1)S(1)}, bf16[64,2048]{1,0:T(8,128)(2,1)S(1)}, u32[]{:S(2)}, u32[]{:S(2)}) collective-permute-start(bf16[64,2048]{1,0:T(8,128)(2,1)S(1)} %fusion.161), channel_id=1, source_target_pairs={{9,7},{10,8},{11,9},{12,10},{13,11},{14,12},{15,13},{1,0},{2,1},{3... | collective-permute-start | bytes 786440 | tf_op jit(solution)/shard_map/ppermute | solution.py:86
  272.8 1.4 collective-permute-start.13
  279.6 14.7 %copy-start.65 = (bf16[2,32,8,128]{3,2,1,0:T(8,128)(2,1)}, bf16[2,32,8,128]{3,2,1,0:T(8,128)(2,1)S(1)}, u32[]{:S(2)}) copy-start(bf16[2,32,8,128]{3,2,1,0:T(8,128)(2,1)S(1)} %copy.383) | copy-start | bytes 393220
  283.4 10.9 %copy-start.122 = (f32[64]{0:T(128)}, f32[64]{0:T(128)S(1)}, u32[]{:S(2)}) copy-start(f32[64]{0:T(128)S(1)} %broadcast_multiply_fusion.7) | copy-start | bytes 772
  284.2 7.7 %collective-permute-start.14 = (bf16[64,2048]{1,0:T(8,128)(2,1)S(1)}, bf16[64,2048]{1,0:T(8,128)(2,1)S(1)}, u32[]{:S(2)}, u32[]{:S(2)}) collective-permute-start(bf16[64,2048]{1,0:T(8,128)(2,1)S(1)} %fusion.162), channel_id=1, source_target_pairs={{9,7},{10,8},{11,9},{12,10},{13,11},{14,12},{15,13},{1,0},{2,1},{3... | collective-permute-start | bytes 786440 | tf_op jit(solution)/shard_map/ppermute | solution.py:86
  291.9 1.5 collective-permute-start.15
  299.0 14.4 %copy-start.66 = (bf16[2,32,8,128]{3,2,1,0:T(8,128)(2,1)}, bf16[2,32,8,128]{3,2,1,0:T(8,128)(2,1)S(1)}, u32[]{:S(2)}) copy-start(bf16[2,32,8,128]{3,2,1,0:T(8,128)(2,1)S(1)} %copy.386) | copy-start | bytes 393220
  302.7 10.7 %copy-start.124 = (f32[64]{0:T(128)}, f32[64]{0:T(128)S(1)}, u32[]{:S(2)}) copy-start(f32[64]{0:T(128)S(1)} %broadcast_multiply_fusion.6) | copy-start | bytes 772
  303.5 7.7 %collective-permute-start.16 = (bf16[64,2048]{1,0:T(8,128)(2,1)S(1)}, bf16[64,2048]{1,0:T(8,128)(2,1)S(1)}, u32[]{:S(2)}, u32[]{:S(2)}) collective-permute-start(bf16[64,2048]{1,0:T(8,128)(2,1)S(1)} %fusion.163), channel_id=1, source_target_pairs={{9,7},{10,8},{11,9},{12,10},{13,11},{14,12},{15,13},{1,0},{2,1},{3... | collective-permute-start | bytes 786440 | tf_op jit(solution)/shard_map/ppermute | solution.py:86
  311.2 1.4 collective-permute-start.17
  318.1 14.5 %copy-start.67 = (bf16[2,32,8,128]{3,2,1,0:T(8,128)(2,1)}, bf16[2,32,8,128]{3,2,1,0:T(8,128)(2,1)S(1)}, u32[]{:S(2)}) copy-start(bf16[2,32,8,128]{3,2,1,0:T(8,128)(2,1)S(1)} %copy.389) | copy-start | bytes 393220
  321.8 10.7 %copy-start.126 = (f32[64]{0:T(128)}, f32[64]{0:T(128)S(1)}, u32[]{:S(2)}) copy-start(f32[64]{0:T(128)S(1)} %broadcast_multiply_fusion.5) | copy-start | bytes 772
  322.7 7.7 %collective-permute-start.18 = (bf16[64,2048]{1,0:T(8,128)(2,1)S(1)}, bf16[64,2048]{1,0:T(8,128)(2,1)S(1)}, u32[]{:S(2)}, u32[]{:S(2)}) collective-permute-start(bf16[64,2048]{1,0:T(8,128)(2,1)S(1)} %fusion.164), channel_id=1, source_target_pairs={{9,7},{10,8},{11,9},{12,10},{13,11},{14,12},{15,13},{1,0},{2,1},{3... | collective-permute-start | bytes 786440 | tf_op jit(solution)/shard_map/ppermute | solution.py:86
  330.3 1.4 collective-permute-start.19
  337.2 16.9 %copy-start.69 = (bf16[2,32,8,128]{3,2,1,0:T(8,128)(2,1)}, bf16[2,32,8,128]{3,2,1,0:T(8,128)(2,1)S(1)}, u32[]{:S(2)}) copy-start(bf16[2,32,8,128]{3,2,1,0:T(8,128)(2,1)S(1)} %copy.392) | copy-start | bytes 393220
  341.0 11.7 %copy-start.128 = (f32[64]{0:T(128)}, f32[64]{0:T(128)S(1)}, u32[]{:S(2)}) copy-start(f32[64]{0:T(128)S(1)} %broadcast_multiply_fusion.4) | copy-start | bytes 772
  341.8 8.3 %collective-permute-start.20 = (bf16[64,2048]{1,0:T(8,128)(2,1)S(1)}, bf16[64,2048]{1,0:T(8,128)(2,1)S(1)}, u32[]{:S(2)}, u32[]{:S(2)}) collective-permute-start(bf16[64,2048]{1,0:T(8,128)(2,1)S(1)} %fusion.165), channel_id=1, source_target_pairs={{9,7},{10,8},{11,9},{12,10},{13,11},{14,12},{15,13},{1,0},{2,1},{3... | collective-permute-start | bytes 786440 | tf_op jit(solution)/shard_map/ppermute | solution.py:86
  350.1 3.2 collective-permute-start.21
  363.4 12.8 %collective-permute-start.22 = (bf16[64,2048]{1,0:T(8,128)(2,1)S(1)}, bf16[64,2048]{1,0:T(8,128)(2,1)}, u32[]{:S(2)}, u32[]{:S(2)}) collective-permute-start(bf16[64,2048]{1,0:T(8,128)(2,1)S(1)} %fusion.166), channel_id=1, source_target_pairs={{9,7},{10,8},{11,9},{12,10},{13,11},{14,12},{15,13},{1,0},{2,1},{3... | collective-permute-start | bytes 786440 | tf_op jit(solution)/shard_map/ppermute | solution.py:86
  376.2 11.1 %collective-permute-start.23 = (bf16[64,2048]{1,0:T(8,128)(2,1)}, bf16[64,2048]{1,0:T(8,128)(2,1)}, u32[]{:S(2)}, u32[]{:S(2)}) collective-permute-start(bf16[64,2048]{1,0:T(8,128)(2,1)} %collective-permute-done.22), channel_id=1, source_target_pairs={{8,9},{10,11},{12,13},{24,25},{26,27},{28,29},{40,41},{42,43},{44,... | collective-permute-start | bytes 786440 | tf_op jit(solution)/shard_map/ppermute | solution.py:87
  399.7 13.0 %collective-permute-start.24 = (bf16[64,2048]{1,0:T(8,128)(2,1)}, bf16[64,2048]{1,0:T(8,128)(2,1)}, u32[]{:S(2)}, u32[]{:S(2)}) collective-permute-start(bf16[64,2048]{1,0:T(8,128)(2,1)} %fusion.167), channel_id=1, source_target_pairs={{9,7},{10,8},{11,9},{12,10},{13,11},{14,12},{15,13},{1,0},{2,1},{3... | collective-permute-start | bytes 786440 | tf_op jit(solution)/shard_map/ppermute | solution.py:86
  412.6 6.9 collective-permute-start.25
  431.8 13.1 %collective-permute-start.26 = (bf16[64,2048]{1,0:T(8,128)(2,1)}, bf16[64,2048]{1,0:T(8,128)(2,1)}, u32[]{:S(2)}, u32[]{:S(2)}) collective-permute-start(bf16[64,2048]{1,0:T(8,128)(2,1)} %fusion.168), channel_id=1, source_target_pairs={{9,7},{10,8},{11,9},{12,10},{13,11},{14,12},{15,13},{1,0},{2,1},{3... | collective-permute-start | bytes 786440 | tf_op jit(solution)/shard_map/ppermute | solution.py:86
  445.0 5.7 collective-permute-start.27
  449.9 9.5 %copy-start.8 = (bf16[64,2048]{1,0:T(8,128)(2,1)S(1)}, bf16[64,2048]{1,0:T(8,128)(2,1)}, u32[]{:S(2)}) copy-start(bf16[64,2048]{1,0:T(8,128)(2,1)} %copy-done.7) | copy-start | bytes 786436
  449.9 9.5 %copy-start.34 = (f32[64,2048]{1,0:T(8,128)S(1)}, f32[64,2048]{1,0:T(8,128)}, u32[]{:S(2)}) copy-start(f32[64,2048]{1,0:T(8,128)} %copy-done.33) | copy-start | bytes 1572868
  449.9 9.5 %copy-start.106 = (f32[64]{0:T(128)S(1)}, f32[64]{0:T(128)}, u32[]{:S(2)}) copy-start(f32[64]{0:T(128)} %get-tuple-element.115) | copy-start | bytes 772
  449.9 9.5 %copy-start.117 = (f32[64]{0:T(128)S(1)}, f32[64]{0:T(128)}, u32[]{:S(2)}) copy-start(f32[64]{0:T(128)} %copy-done.116) | copy-start | bytes 772
  451.8 9.6 %copy-start.12 = (bf16[64,2048]{1,0:T(8,128)(2,1)S(1)}, bf16[64,2048]{1,0:T(8,128)(2,1)}, u32[]{:S(2)}) copy-start(bf16[64,2048]{1,0:T(8,128)(2,1)} %copy-done.11) | copy-start | bytes 786436
  451.9 9.6 %copy-start.38 = (f32[64,2048]{1,0:T(8,128)S(1)}, f32[64,2048]{1,0:T(8,128)}, u32[]{:S(2)}) copy-start(f32[64,2048]{1,0:T(8,128)} %copy-done.37) | copy-start | bytes 1572868
  451.9 9.6 %copy-start.102 = (f32[64]{0:T(128)S(1)}, f32[64]{0:T(128)}, u32[]{:S(2)}) copy-start(f32[64]{0:T(128)} %get-tuple-element.113) | copy-start | bytes 772
  451.9 9.6 %copy-start.121 = (f32[64]{0:T(128)S(1)}, f32[64]{0:T(128)}, u32[]{:S(2)}) copy-start(f32[64]{0:T(128)} %copy-done.120) | copy-start | bytes 772
  454.2 15.1 %copy-start.56 = (bf16[64,2048]{1,0:T(8,128)(2,1)}, bf16[64,2048]{1,0:T(8,128)(2,1)S(1)}, u32[]{:S(2)}) copy-start(bf16[64,2048]{1,0:T(8,128)(2,1)S(1)} %get-tuple-element.73) | copy-start | bytes 786436
  (106 other events, 595.5 us)
Sparse Core Ops, SparseCore 0:
  10.4 122.6 all-gather.1
  493.8 144.1 reduce-scatter.2
